TPU v7x, 512 devices: a whole 4x4x16 slice. The times are simulated.
512 devices in a mesh: replica: 64 (over x, z), head: 8 (over y, core).
Axes of the slice: x: 4, y: 4, z: 16, core: 2. Of those that a mesh axis runs over, the one named last changes fastest.
Arguments:
- states: float32 [256, 32, 128, 128], P('replica', 'head'), may hold values from -18 to 18
- partner: int32 [64], replicated, may hold values from 0 to 63, as said below
- send_ids: int32 [64, 2], replicated, may hold values from 0 to 3, as said below
- send_count: int32 [64], replicated, may hold values from 1 to 2, as said below
- prefill_slot: int32 [64], P('replica'), may hold values from 0 to 3
- prompt_len: int32 [64], P('replica'), may hold values from 128 to 512, as said below
- decode_slots: int32 [64, 4], P('replica'), may hold values from 0 to 3, each once within a row
- q_prefill: bfloat16 [32768, 4096], P('replica', 'head'), may hold values from -6 to 6
- k_prefill: bfloat16 [32768, 4096], P('replica', 'head'), may hold values from -6 to 6
- v_prefill: bfloat16 [32768, 4096], P('replica', 'head'), may hold values from -6 to 6
- q_decode: bfloat16 [2, 256, 4096], P(None, 'replica', 'head'), may hold values from -6 to 6
- k_decode: bfloat16 [2, 256, 4096], P(None, 'replica', 'head'), may hold values from -6 to 6
- v_decode: bfloat16 [2, 256, 4096], P(None, 'replica', 'head'), may hold values from -6 to 6
- slopes: float32 [32], P('head'), may hold values from 0.003 to 0.06
- w_out: bfloat16 [4096, 3072], P('head'), may hold values from -0.125 to 0.125
Outputs:
- prefill_out: bfloat16 [32768, 3072], P('replica', 'head')
- decode_out: bfloat16 [2, 256, 3072], P(None, 'replica', 'head')
Inputs may be any that keep to these rules, and one draw needn't show every extreme that they name: partner[i] = i XOR m for one number m with 1 <= m < 64, the same for every replica, so replicas form pairs. `send_ids`: each row names 2 different slots. `send_count`: some replica sends 2 requests in every draw. `prompt_len`: some replica has 512 valid tokens in every draw.
All inputs are finite; a program needn't handle non-finite values.
Results may differ from a plain program's by a relative error of at most 0.017.
Values may be sent and summed in bfloat16 or wider, within the bound.
No kernel may reach another device: no remote copies, remote signals or barrier semaphores. Data moves between devices by JAX's collectives and lax.ppermute only.
A program may use at most 64 MiB of HBM per device.

v0:
```python
from functools import partial

import jax
import jax.numpy as jnp
from jax import lax
from jax.experimental import pallas as pl
from jax.experimental.pallas import tpu as pltpu
from jax.sharding import PartitionSpec as P

DK = 128
BLK = 128
EPS = 1e-06
PAD = 16
VMEM_LIMIT = 48 * 1024 * 1024
ORDER = (2, 1, 3, 0)


def params(axes=1):
    return pltpu.CompilerParams(
        dimension_semantics=("arbitrary",) * axes, vmem_limit_bytes=VMEM_LIMIT
    )


def dot(left, right, left_dim=1, right_dim=0):
    return lax.dot_general(
        left, right, (((left_dim,), (right_dim,)), ((), ())), preferred_element_type=jnp.float32
    )


def split_dot(left, right):
    high = right.astype(jnp.bfloat16)
    low = (right - high.astype(jnp.float32)).astype(jnp.bfloat16)
    return dot(left, high) + dot(left, low)


def pack_kernel(own_ref, ids_ref, states_ref, out_ref):
    out_ref[...] = states_ref[...].astype(jnp.bfloat16)


def pack(own, send_ids, states):
    _, heads, rows, cols = states.shape
    count = send_ids.shape[0]
    block = (1, heads, rows, cols)
    return pl.pallas_call(
        pack_kernel,
        out_shape=jax.ShapeDtypeStruct((count, heads, rows, cols), jnp.bfloat16),
        grid_spec=pltpu.PrefetchScalarGridSpec(
            num_scalar_prefetch=2,
            grid=(count,),
            in_specs=[pl.BlockSpec(block, lambda j, own, ids: (ids[j, own[0]], 0, 0, 0))],
            out_specs=pl.BlockSpec(block, lambda j, own, ids: (j, 0, 0, 0)),
        ),
        compiler_params=params(),
        name="pack",
    )(own, send_ids, states)


def copy_kernel(in_ref, out_ref):
    out_ref[...] = in_ref[...]


def copied(array):
    return pl.pallas_call(
        copy_kernel,
        out_shape=jax.ShapeDtypeStruct(array.shape, array.dtype),
        compiler_params=params(0),
        name="copied",
    )(array)


def head_norm(inputs):
    return inputs * lax.rsqrt(jnp.mean(inputs * inputs, axis=-1, keepdims=True) + EPS)


def fade_row(exponent):
    return jnp.exp(jnp.full((1, DK), exponent))


def decode_rows(ref):
    return jnp.concatenate([ref[step].astype(jnp.float32) for step in range(ref.shape[0])], axis=0)


def own_kernel(
    place_ref, partner_ref, ids_ref, count_ref, slot_ref, len_ref, decode_ref, slopes_ref,
    states_ref, q_ref, k_ref, v_ref, qd_ref, kd_ref, vd_ref, mine_ref, theirs_ref,
    att_ref, dec_ref, mine_out_ref, theirs_out_ref, mem_ref,
):
    mine_out_ref[0] = mine_ref[...]
    theirs_out_ref[0] = theirs_ref[...]
    slope = slopes_ref[pl.program_id(0)]
    own = place_ref[0]
    mate = partner_ref[own]
    length = len_ref[0]
    prefill_slot = slot_ref[0]

    def kept(slot):
        gone = jnp.bool_(False)
        for entry in range(ids_ref.shape[0]):
            gone |= (ids_ref[entry, own] == slot) & (entry < count_ref[own])
            gone |= (ids_ref[entry, mate] == slot) & (entry < count_ref[mate])
        return jnp.where(gone, 0.0, states_ref[slot, 0])

    rows = lax.broadcasted_iota(jnp.int32, (BLK, BLK), 0)
    cols = lax.broadcasted_iota(jnp.int32, (BLK, BLK), 1)
    damping = jnp.exp(-slope * jnp.maximum(rows - cols, 0).astype(jnp.float32))
    leading = jnp.exp(-slope * (rows + 1).astype(jnp.float32))
    mem_ref[...] = kept(prefill_slot)

    def step(block, carry):
        count = jnp.clip(length - block * BLK, 0, BLK)
        here = pl.ds(pl.multiple_of(block * BLK, BLK), BLK)
        q_block, k_block, v_block = q_ref[here, :], k_ref[here, :], v_ref[here, :]
        memory = mem_ref[...]
        scores = dot(q_block, k_block, 1, 1)
        valid = (cols <= rows) & (cols < count)
        probs = jnp.where(valid, scores * damping, 0.0).astype(jnp.bfloat16)
        att_ref[here, :] = dot(probs, v_block) + leading * split_dot(q_block, memory)
        behind = jnp.maximum(count - 1 - rows, 0).astype(jnp.float32)
        trailing = jnp.where(rows < count, jnp.exp(-slope * behind), 0.0)
        weighted = (k_block.astype(jnp.float32) * trailing).astype(jnp.bfloat16)
        mem_ref[...] = fade_row(-slope * count.astype(jnp.float32)) * memory + dot(
            weighted, v_block, 0, 0
        )
        return carry

    lax.fori_loop(0, q_ref.shape[0] // BLK, step, 0)

    keep = fade_row(-slope)
    slots = decode_ref.shape[1]
    queries, keys, values = (decode_rows(ref) for ref in (qd_ref, kd_ref, vd_ref))
    padded = jnp.concatenate([queries, queries], axis=0).astype(jnp.bfloat16)
    place = lax.broadcasted_iota(jnp.int32, (2 * slots, DK), 0)
    seen = jnp.zeros((2 * slots, DK), jnp.float32)
    for row in range(slots):
        slot = decode_ref[0, row]
        memory = jnp.where(slot == prefill_slot, mem_ref[...], kept(slot))
        seen = jnp.where(place % slots == row, split_dot(padded, memory)[: 2 * slots], seen)
    product = lambda q, k: jnp.sum(q * k, axis=-1, keepdims=True)
    first, second = slice(0, slots), slice(slots, 2 * slots)
    now = product(queries, keys) * values
    before = product(queries[second], keys[first]) * values[first]
    dec_ref[first, :] = keep * seen[first] + now[first]
    dec_ref[second, :] = keep * (keep * seen[second] + before) + now[second]


def far_chip(place, step):
    away = jnp.where(
        step == 0, ORDER[0], jnp.where(step == 1, ORDER[1], jnp.where(step == 2, ORDER[2], ORDER[3]))
    )
    return lax.rem(place[1] // 2 + away, 4)


def own_part(place, scalars, states, prefill, decode, w_out):
    slots, heads = states.shape[:2]
    tokens, width = prefill[0].shape
    cols = w_out.shape[1] // 8
    steps = decode[0].shape[0]
    column = pl.BlockSpec((tokens, DK), lambda h, *_: (0, h))
    row = pl.BlockSpec((steps, slots, DK), lambda h, *_: (0, 0, h))
    taken = pl.BlockSpec((1, width, cols), lambda h, *_: (h, 0, 0))

    def weights(other):
        def index(h, place, *_):
            core = lax.rem(place[1], 2)
            return (0, 2 * far_chip(place, h) + (1 - core if other else core))

        return pl.BlockSpec((width, cols), index)

    return pl.pallas_call(
        own_kernel,
        out_shape=(
            jax.ShapeDtypeStruct((tokens, width), jnp.float32),
            jax.ShapeDtypeStruct((steps * slots, width), jnp.float32),
            jax.ShapeDtypeStruct((4, width, cols), jnp.bfloat16),
            jax.ShapeDtypeStruct((4, width, cols), jnp.bfloat16),
        ),
        grid_spec=pltpu.PrefetchScalarGridSpec(
            num_scalar_prefetch=8,
            grid=(heads,),
            in_specs=[
                pl.BlockSpec((slots, 1, DK, DK), lambda h, *_: (0, h, 0, 0)),
                column,
                column,
                column,
                row,
                row,
                row,
                weights(False),
                weights(True),
            ],
            out_specs=(
                column,
                pl.BlockSpec((steps * slots, DK), lambda h, *_: (0, h)),
                taken,
                taken,
            ),
            scratch_shapes=[pltpu.VMEM((DK, DK), jnp.float32)],
        ),
        compiler_params=params(),
        cost_estimate=pl.CostEstimate(
            flops=10 * tokens * BLK * width,
            bytes_accessed=5 * tokens * width * 2 + 4 * w_out.size,
            transcendentals=0,
        ),
        name="own_part",
    )(place, *scalars, states, *prefill, *decode, w_out, w_out)


def serve_kernel(
    place_ref, partner_ref, ids_ref, count_ref, slot_ref, len_ref, decode_ref, slopes_ref,
    payload_ref, att_ref, dec_ref, q_ref, qd_ref, normed_ref,
):
    tokens, width = q_ref.shape
    mate = partner_ref[place_ref[0]]
    prefill_slot = slot_ref[0]
    length = len_ref[0]
    slots = decode_ref.shape[1]
    entries = ids_ref.shape[0]
    lands = [
        lambda slot, e=e: ((ids_ref[e, mate] == slot) & (e < count_ref[mate])) for e in range(entries)
    ]
    rows = lax.broadcasted_iota(jnp.int32, (tokens, DK), 0)
    place = lax.broadcasted_iota(jnp.int32, (2 * slots, DK), 0)
    later = (rows + 1).astype(jnp.float32)
    is_valid = rows < length
    for head in range(width // DK):
        here = slice(head * DK, (head + 1) * DK)
        slope = slopes_ref[head]
        chosen = jnp.zeros((DK, DK), jnp.bfloat16)
        for entry in range(entries):
            chosen = jnp.where(lands[entry](prefill_slot), payload_ref[entry, head], chosen)
        attended = att_ref[:, here] + jnp.exp(-slope * later) * dot(q_ref[:, here], chosen)
        normed = jnp.where(is_valid, head_norm(attended), 0.0)
        normed_ref[:tokens, here] = normed.astype(jnp.bfloat16)

        keep = fade_row(-slope)
        faded = fade_row(-slope * length.astype(jnp.float32))
        queries = decode_rows(qd_ref.at[:, :, here])
        padded = jnp.concatenate([queries, queries], axis=0).astype(jnp.bfloat16)
        scale = jnp.where(place < slots, keep, keep * keep)
        decoded = dec_ref[:, here]
        for entry in range(entries):
            seen = dot(padded, payload_ref[entry, head])[: 2 * slots]
            share = jnp.zeros((2 * slots, DK), jnp.float32)
            for row in range(slots):
                slot = decode_ref[0, row]
                factor = jnp.where(slot == prefill_slot, faded, 1.0)
                factor = jnp.where(lands[entry](slot), factor, 0.0)
                share = jnp.where(place % slots == row, factor, share)
            decoded += scale * share * seen
        decoded = head_norm(decoded)
        padding = jnp.zeros((PAD - 2 * slots, DK), jnp.float32)
        decoded = jnp.concatenate([decoded, padding], axis=0)
        normed_ref[tokens:, here] = decoded.astype(jnp.bfloat16)


def serve(place, scalars, payload, attended, decoded, q_prefill, q_decode):
    tokens, width = q_prefill.shape
    scalar = pl.BlockSpec(memory_space=pltpu.SMEM)
    whole = pl.BlockSpec(memory_space=pltpu.VMEM)
    return pl.pallas_call(
        serve_kernel,
        out_shape=jax.ShapeDtypeStruct((tokens + PAD, width), jnp.bfloat16),
        in_specs=[scalar] * 8 + [whole] * 5,
        out_specs=whole,
        compiler_params=params(0),
        name="serve",
    )(place, *scalars, payload, attended, decoded, q_prefill, q_decode)


def join_kernel(own_ref, other_ref, *refs):
    count = len(refs) // 3
    for mine_ref, theirs_ref, out_ref in zip(refs[:count], refs[count : 2 * count], refs[2 * count :]):
        total = dot(own_ref[...], mine_ref[0]) + dot(other_ref[...], theirs_ref[0])
        out_ref[...] = total.astype(jnp.bfloat16)


def join(own, other, mine, theirs, chips):
    whole = pl.BlockSpec(memory_space=pltpu.VMEM)
    count = len(chips)
    shape = (own.shape[0], mine.shape[2])
    blocks = [pl.BlockSpec((1, *mine.shape[1:]), lambda i, chip=chip: (chip, 0, 0)) for chip in chips]
    return pl.pallas_call(
        join_kernel,
        out_shape=(jax.ShapeDtypeStruct(shape, jnp.bfloat16),) * count,
        grid=(1,),
        in_specs=[whole] * 2 + blocks * 2,
        out_specs=(whole,) * count,
        compiler_params=params(),
        name=f"join{chips[0]}",
        cost_estimate=pl.CostEstimate(
            flops=4 * count * own.size * mine.shape[2],
            bytes_accessed=4 * own.size + 4 * count * mine.shape[1] * mine.shape[2],
            transcendentals=0,
        ),
    )(own, other, *[mine] * count, *[theirs] * count)


def add_kernel(a_ref, b_ref, out_ref):
    out_ref[...] = a_ref[...].astype(jnp.float32) + b_ref[...].astype(jnp.float32)


def add(a, b):
    return pl.pallas_call(
        add_kernel,
        out_shape=jax.ShapeDtypeStruct(a.shape, jnp.float32),
        compiler_params=params(0),
        name="add",
    )(a, b)


def finish_kernel(a_ref, b_ref, c_ref, prefill_ref, decode_ref):
    total = a_ref[...] + b_ref[...].astype(jnp.float32) + c_ref[...].astype(jnp.float32)
    tokens = prefill_ref.shape[0]
    prefill_ref[...] = total[:tokens].astype(jnp.bfloat16)
    steps, slots, _ = decode_ref.shape
    for step in range(steps):
        first = tokens + step * slots
        decode_ref[step] = total[first : first + slots].astype(jnp.bfloat16)


def finish(total, near, tokens, steps, slots):
    cols = total.shape[1]
    return pl.pallas_call(
        finish_kernel,
        out_shape=(
            jax.ShapeDtypeStruct((tokens, cols), jnp.bfloat16),
            jax.ShapeDtypeStruct((steps, slots, cols), jnp.bfloat16),
        ),
        compiler_params=params(0),
        name="finish",
    )(total, *near)


def siblings():
    return [(i, i ^ 1) for i in range(lax.axis_size("head"))]


def swapped(partner, array):
    return lax.cond(
        partner[0] >= 0, lambda own: lax.ppermute(own, "head", siblings()), jnp.zeros_like, array
    )


def exchange(array, pattern):
    size = lax.axis_size("replica")
    return lax.ppermute(array, "replica", [(i, i ^ pattern) for i in range(size)])


def on_device(
    states,
    partner,
    send_ids,
    send_count,
    prefill_slot,
    prompt_len,
    decode_slots,
    q_prefill,
    k_prefill,
    v_prefill,
    q_decode,
    k_decode,
    v_decode,
    slopes,
    w_out,
):
    size = lax.axis_size("replica")
    own = lax.axis_index("replica")
    head = lax.axis_index("head")
    place = jnp.stack([own, head]).astype(jnp.int32)
    ids = send_ids.T
    scalars = (partner, ids, send_count, prefill_slot, prompt_len, decode_slots, slopes)
    devices = lax.axis_size("head")

    pattern = jnp.clip(partner[0], 1, size - 1)
    half, across = size // 2, size // 4 * 3

    def hop(*arrays):
        return exchange(pack(*arrays), across)

    payload = lax.cond(pattern >= half, hop, pack, place, ids, states)

    def branch(rest, payload, *arrays):
        moving = exchange(payload, rest) if rest else copied(payload)
        attended, decoded, mine, theirs = own_part(*arrays)
        return moving, attended, decoded, mine, swapped(partner, theirs)

    payload, attended, decoded, mine, theirs = lax.switch(
        jnp.where(pattern >= half, pattern ^ across, pattern),
        [partial(branch, rest) for rest in range(half)],
        payload,
        place,
        scalars,
        states,
        (q_prefill, k_prefill, v_prefill),
        (q_decode, k_decode, v_decode),
        w_out,
    )
    normed = serve(place, scalars, payload, attended, decoded, q_prefill, q_decode)
    other = lax.ppermute(normed, "head", siblings())

    def along(part, away):
        return lax.ppermute(part, "head", [(i, (i + 2 * away) % devices) for i in range(devices)])

    (farthest,) = join(normed, other, mine, theirs, (0,))
    farthest, normed = lax.optimization_barrier((farthest, normed))
    *near, here = join(normed, other, mine, theirs, (1, 2, 3))
    near = [along(part, away) for part, away in zip(near, ORDER[1:-1], strict=True)]
    total = add(along(farthest, ORDER[0]), here)
    steps, slots = q_decode.shape[:2]
    return finish(total, near, q_prefill.shape[0], steps, slots)


def solution(mesh):
    return jax.shard_map(
        on_device,
        mesh=mesh,
        in_specs=(
            P("replica", "head", None, None),
            P(),
            P(),
            P(),
            P("replica"),
            P("replica"),
            P("replica", None),
            P("replica", "head"),
            P("replica", "head"),
            P("replica", "head"),
            P(None, "replica", "head"),
            P(None, "replica", "head"),
            P(None, "replica", "head"),
            P("head"),
            P("head", None),
        ),
        out_specs=(P("replica", "head"), P(None, "replica", "head")),
        check_vma=False,
    )
```

profile of v0, /device:TPU:88, one launch (start us, length us, event | category | flops | bytes accessed | tf_op | source)
XLA Modules:
  0.0 77.8 jit_solution(8811477458650402037)
XLA Ops:
  0.6 0.0 copy-start.6
  0.6 0.0 copy-start.7
  0.7 0.0 copy-start.8
  0.7 0.0 copy-start
  0.7 0.0 copy-start.1
  0.7 0.0 copy-start.2
  0.7 0.0 copy-start.3
  0.7 0.0 copy-start.4
  0.7 0.0 copy-start.5
  0.7 0.0 copy-start.9
  2.8 0.1 pad_add_fusion.place_ref
  2.9 13.0 %conditional.34 = (bf16[2,4,128,128]{3,2,1,0:T(8,128)(2,1)}) conditional(s32[]{:T(128)} %convert_element_type.195, (s32[2]{0:T(128)S(1)}, s32[2,64]{1,0:T(2,128)}, f32[4,4,128,128]{3,2,1,0:T(8,128)}) %tuple.627, (s32[2]{0:T(128)S(1)}, s32[2,64]{1,0:T(2,128)}, f32[4,4,128,128]{3,2,1,0:T(8,128)}) %tuple.628), branch_computations={%region_0.1_spmd, %region_1.2_spmd} | conditional | bytes 1048624 | solution.py:381
  2.9 1.8 %pack.3 = bf16[2,4,128,128]{3,2,1,0:T(8,128)(2,1)S(1)} custom-call(s32[2]{0:T(128)S(1)} %get-tuple-element.1234.own_ref, s32[2,64]{1,0:T(2,128)} %get-tuple-element.1235.ids_ref, f32[4,4,128,128]{3,2,1,0:T(8,128)} %get-tuple-element.1236.states_ref), custom_call_target="tpu_custom_call" | custom-call | tf_op jit(solution)/shard_map/cond/branch_1_fun/pack/pallas_call | solution.py:44
  4.7 4.7 %collective-permute-start = (bf16[2,4,128,128]{3,2,1,0:T(8,128)(2,1)S(1)}, bf16[2,4,128,128]{3,2,1,0:T(8,128)(2,1)}, u32[]{:S(2)}, u32[]{:S(2)}) collective-permute-start(bf16[2,4,128,128]{3,2,1,0:T(8,128)(2,1)S(1)} %pack.3), channel_id=1, source_target_pairs={{0,384},{8,392},{16,400},{24,408},{32,416},{40,424},{48,432},{56,4... | collective-permute-start | bytes 786440 | tf_op jit(solution)/shard_map/cond/branch_1_fun/ppermute | solution.py:347
  9.3 6.6 %collective-permute-done = bf16[2,4,128,128]{3,2,1,0:T(8,128)(2,1)} collective-permute-done((bf16[2,4,128,128]{3,2,1,0:T(8,128)(2,1)S(1)}, bf16[2,4,128,128]{3,2,1,0:T(8,128)(2,1)}, u32[]{:S(2)}, u32[]{:S(2)}) %collective-permute-start) | collective-permute-done | bytes 262176 | tf_op jit(solution)/shard_map/cond/branch_1_fun/ppermute | solution.py:347
  15.9 0.0 copy-done.6
  15.9 0.0 copy-done.7
  15.9 0.0 copy-done.8
  15.9 0.0 copy-done
  15.9 0.0 copy-done.1
  16.0 0.0 copy-done.2
  16.0 0.0 copy-done.3
  16.0 0.0 copy-done.4
  16.0 0.0 copy-done.5
  16.0 0.0 copy-done.9
  16.0 29.0 %conditional.35 = (bf16[2,4,128,128]{3,2,1,0:T(8,128)(2,1)}, f32[512,512]{1,0:T(8,128)}, f32[8,512]{1,0:T(8,128)S(1)}, bf16[4,512,384]{2,1,0:T(8,128)(2,1)S(1)}, bf16[4,512,384]{2,1,0:T(8,128)(2,1)}) conditional(s32[]{:T(128)} %clamp.3, (bf16[2,4,128,128]{3,2,1,0:T(8,128)(2,1)}, s32[2]{0:T(128)S(1)}, ...), branch_computations={%region_2.5_spmd, %region_5.8_spmd, %region_8.11_spmd, %region_11.... | conditional | flops 335544320 | bytes 16253070 | solution.py:388
  16.0 6.4 %collective-permute-start.13 = (bf16[2,4,128,128]{3,2,1,0:T(8,128)(2,1)}, bf16[2,4,128,128]{3,2,1,0:T(8,128)(2,1)}, u32[]{:S(2)}, u32[]{:S(2)}) collective-permute-start(bf16[2,4,128,128]{3,2,1,0:T(8,128)(2,1)} %get-tuple-element.1363), channel_id=1, source_target_pairs={{0,48},{8,56},{16,32},{24,40},{32,16},{40,24},{48,0},{56,8},{64,11... | collective-permute-start | bytes 786440 | tf_op jit(solution)/shard_map/cond/branch_6_fun/ppermute | solution.py:347
  22.5 10.2 %own_part.38 = (f32[512,512]{1,0:T(8,128)}, f32[8,512]{1,0:T(8,128)S(1)}, bf16[4,512,384]{2,1,0:T(8,128)(2,1)S(1)}, bf16[4,512,384]{2,1,0:T(8,128)(2,1)}) custom-call(s32[2]{0:T(128)S(1)} %get-tuple-element.1364.place_ref, s32[64]{0:T(128)S(1)} %get-tuple-element.1365.partner_ref, s32[2,64]{1,0:T(2,128)} %get-tuple-element.1366.ids_ref, ...), custom_call_target="tpu_custom_call" | custom-call | flops 335544320 | bytes 8912896 | tf_op jit(solution)/shard_map/cond/branch_6_fun/own_part/pallas_call | solution.py:169
  32.7 5.6 %conditional.6 = (bf16[4,512,384]{2,1,0:T(8,128)(2,1)}) conditional(s32[]{:T(128)} %bitcast.6, () %tuple.246, bf16[4,512,384]{2,1,0:T(8,128)(2,1)} %get-tuple-element.1383), branch_computations={%region_21.21_spmd, %region_22.22_spmd} | conditional | bytes 6291504 | solution.py:340
  32.7 1.9 %collective-permute-start.12 = (bf16[4,512,384]{2,1,0:T(8,128)(2,1)}, bf16[4,512,384]{2,1,0:T(8,128)(2,1)}, u32[]{:S(2)}, u32[]{:S(2)}) collective-permute-start(bf16[4,512,384]{2,1,0:T(8,128)(2,1)} %param.21), channel_id=1, source_target_pairs={{0,1},{1,0},{2,3},{3,2},{4,5},{5,4},{6,7},{7,6},{8,9},{9,8},{10,11... | collective-permute-start | bytes 4718600 | tf_op jit(solution)/shard_map/cond/branch_6_fun/cond/branch_1_fun/ppermute | solution.py:341
  34.6 3.7 %collective-permute-done.12 = bf16[4,512,384]{2,1,0:T(8,128)(2,1)} collective-permute-done((bf16[4,512,384]{2,1,0:T(8,128)(2,1)}, bf16[4,512,384]{2,1,0:T(8,128)(2,1)}, u32[]{:S(2)}, u32[]{:S(2)}) %collective-permute-start.12) | collective-permute-done | bytes 1572896 | tf_op jit(solution)/shard_map/cond/branch_6_fun/cond/branch_1_fun/ppermute | solution.py:341
  38.3 6.7 %collective-permute-done.13 = bf16[2,4,128,128]{3,2,1,0:T(8,128)(2,1)} collective-permute-done((bf16[2,4,128,128]{3,2,1,0:T(8,128)(2,1)}, bf16[2,4,128,128]{3,2,1,0:T(8,128)(2,1)}, u32[]{:S(2)}, u32[]{:S(2)}) %collective-permute-start.13) | collective-permute-done | bytes 262176 | tf_op jit(solution)/shard_map/cond/branch_6_fun/ppermute | solution.py:347
  45.0 2.0 %serve.1.own_ref = bf16[528,512]{1,0:T(8,128)(2,1)S(1)} custom-call(s32[2]{0:T(128)S(1)} %pad_add_fusion.place_ref, s32[64]{0:T(128)S(1)} %copy-done.6, s32[2,64]{1,0:T(2,128)} %bitcast.103, s32[64]{0:T(128)S(1)} %copy-done.7, s32[1]{0:T(128)S(6)} %copy.243.slot_ref, s32[1]{0:T(128)S(6)} %copy.244.len_ref, s32[1,4]{1,0:T(1,128)S(1)} %copy-done.8, ...), custom_call_target="tpu_custom_call" | custom-call | tf_op jit(solution)/shard_map/serve/pallas_call | solution.py:261
  47.0 1.9 %collective-permute-start.64 = (bf16[528,512]{1,0:T(8,128)(2,1)S(1)}, bf16[528,512]{1,0:T(8,128)(2,1)S(1)}, u32[]{:S(2)}, u32[]{:S(2)}) collective-permute-start(bf16[528,512]{1,0:T(8,128)(2,1)S(1)} %serve.1.own_ref), channel_id=1, source_target_pairs={{0,1},{1,0},{2,3},{3,2},{4,5},{5,4},{6,7},{7,6},{8,9},{9,8},{10,11... | collective-permute-start | bytes 1622024 | tf_op jit(solution)/shard_map/ppermute | solution.py:400
  49.0 1.9 %collective-permute-done.64.other_ref = bf16[528,512]{1,0:T(8,128)(2,1)S(1)} collective-permute-done((bf16[528,512]{1,0:T(8,128)(2,1)S(1)}, bf16[528,512]{1,0:T(8,128)(2,1)S(1)}, u32[]{:S(2)}, u32[]{:S(2)}) %collective-permute-start.64) | collective-permute-done | bytes 540704 | tf_op jit(solution)/shard_map/ppermute | solution.py:400
  50.9 1.7 %join0.1 = bf16[528,384]{1,0:T(8,128)(2,1)S(1)} custom-call(bf16[528,512]{1,0:T(8,128)(2,1)S(1)} %serve.1.own_ref, bf16[528,512]{1,0:T(8,128)(2,1)S(1)} %collective-permute-done.64.other_ref, bf16[4,512,384]{2,1,0:T(8,128)(2,1)S(1)} %get-tuple-element.1924.refs_0_.refs_1_.refs_2_, bf16[4,512,384]{2,1,0:T(8,128)(2,1)} %get-tuple-element.1925.refs_1_.refs_3_.refs_4_.refs_5_), custom_call_target="tpu_custom_call" | custom-call | flops 415236096 | bytes 1867776 | tf_op jit(solution)/shard_map/join0/pallas_call | solution.py:283
  52.6 3.1 %collective-permute-start.65 = (bf16[528,384]{1,0:T(8,128)(2,1)S(1)}, bf16[528,384]{1,0:T(8,128)(2,1)S(1)}, u32[]{:S(2)}, u32[]{:S(2)}) collective-permute-start(bf16[528,384]{1,0:T(8,128)(2,1)S(1)} %join0.1), channel_id=1, source_target_pairs={{0,4},{1,5},{2,6},{3,7},{4,0},{5,1},{6,2},{7,3},{8,12},{9,13},{10,... | collective-permute-start | bytes 1216520 | tf_op jit(solution)/shard_map/ppermute | solution.py:403
  55.7 3.1 %join1.1 = (bf16[528,384]{1,0:T(8,128)(2,1)S(1)}, bf16[528,384]{1,0:T(8,128)(2,1)S(1)}, bf16[528,384]{1,0:T(8,128)(2,1)S(1)}) custom-call(bf16[528,512]{1,0:T(8,128)(2,1)S(1)} %serve.1.own_ref, bf16[528,512]{1,0:T(8,128)(2,1)S(1)} %collective-permute-done.64.other_ref, bf16[4,512,384]{2,1,0:T(8,128)(2,1)S(1)} %get-tuple-element.1924.refs_0_.refs_1_.refs_2_, ...), custom_call_target="tpu_custom_call" | custom-call | flops 1245708288 | bytes 3440640 | tf_op jit(solution)/shard_map/join1/pallas_call | solution.py:283
  58.8 4.1 %collective-permute-start.66 = (bf16[528,384]{1,0:T(8,128)(2,1)S(1)}, bf16[528,384]{1,0:T(8,128)(2,1)S(1)}, u32[]{:S(2)}, u32[]{:S(2)}) collective-permute-start(bf16[528,384]{1,0:T(8,128)(2,1)S(1)} %get-tuple-element.1929), channel_id=1, source_target_pairs={{0,2},{1,3},{2,4},{3,5},{4,6},{5,7},{6,0},{7,1},{8,10},{9,11},{10,... | collective-permute-start | bytes 1216520 | tf_op jit(solution)/shard_map/ppermute | solution.py:403
  62.9 1.9 %collective-permute-start.67 = (bf16[528,384]{1,0:T(8,128)(2,1)S(1)}, bf16[528,384]{1,0:T(8,128)(2,1)S(1)}, u32[]{:S(2)}, u32[]{:S(2)}) collective-permute-start(bf16[528,384]{1,0:T(8,128)(2,1)S(1)} %get-tuple-element.1930), channel_id=1, source_target_pairs={{0,6},{1,7},{2,0},{3,1},{4,2},{5,3},{6,4},{7,5},{8,14},{9,15},{10,... | collective-permute-start | bytes 1216520 | tf_op jit(solution)/shard_map/ppermute | solution.py:403
  64.9 2.8 %collective-permute-done.65.a_ref = bf16[528,384]{1,0:T(8,128)(2,1)S(1)} collective-permute-done((bf16[528,384]{1,0:T(8,128)(2,1)S(1)}, bf16[528,384]{1,0:T(8,128)(2,1)S(1)}, u32[]{:S(2)}, u32[]{:S(2)}) %collective-permute-start.65) | collective-permute-done | bytes 405536 | tf_op jit(solution)/shard_map/ppermute | solution.py:403
  67.6 0.1 add.3.a_ref
  67.7 5.9 %collective-permute-done.66.b_ref = bf16[528,384]{1,0:T(8,128)(2,1)S(1)} collective-permute-done((bf16[528,384]{1,0:T(8,128)(2,1)S(1)}, bf16[528,384]{1,0:T(8,128)(2,1)S(1)}, u32[]{:S(2)}, u32[]{:S(2)}) %collective-permute-start.66) | collective-permute-done | bytes 405536 | tf_op jit(solution)/shard_map/ppermute | solution.py:403
  73.7 3.2 %collective-permute-done.67.c_ref = bf16[528,384]{1,0:T(8,128)(2,1)S(1)} collective-permute-done((bf16[528,384]{1,0:T(8,128)(2,1)S(1)}, bf16[528,384]{1,0:T(8,128)(2,1)S(1)}, u32[]{:S(2)}, u32[]{:S(2)}) %collective-permute-start.67) | collective-permute-done | bytes 405536 | tf_op jit(solution)/shard_map/ppermute | solution.py:403
  76.9 0.9 %finish.1 = (bf16[512,384]{1,0:T(8,128)(2,1)}, bf16[2,4,384]{2,1,0:T(4,128)(2,1)}) custom-call(f32[528,384]{1,0:T(8,128)S(1)} %add.3.a_ref, bf16[528,384]{1,0:T(8,128)(2,1)S(1)} %collective-permute-done.66.b_ref, bf16[528,384]{1,0:T(8,128)(2,1)S(1)} %collective-permute-done.67.c_ref), custom_call_target="tpu_custom_call" | custom-call | tf_op jit(solution)/shard_map/finish/pallas_call | solution.py:324
Async XLA Ops:
  0.6 15.3 %copy-start.6 = (s32[64]{0:T(128)S(1)}, s32[64]{0:T(128)}, u32[]{:S(2)}) copy-start(s32[64]{0:T(128)} %partner_ref.1) | copy-start | bytes 772
  0.6 15.3 %copy-start.7 = (s32[64]{0:T(128)S(1)}, s32[64]{0:T(128)}, u32[]{:S(2)}) copy-start(s32[64]{0:T(128)} %count_ref.1) | copy-start | bytes 772
  0.7 15.3 %copy-start.8 = (s32[1,4]{1,0:T(1,128)S(1)}, s32[1,4]{1,0:T(1,128)}, u32[]{:S(2)}) copy-start(s32[1,4]{1,0:T(1,128)} %decode_ref.1) | copy-start | bytes 52
  0.7 15.3 %copy-start = (bf16[512,512]{1,0:T(8,128)(2,1)S(1)}, bf16[512,512]{1,0:T(8,128)(2,1)}, u32[]{:S(2)}) copy-start(bf16[512,512]{1,0:T(8,128)(2,1)} %q_ref.1) | copy-start | bytes 1572868
  0.7 15.3 %copy-start.1 = (bf16[512,512]{1,0:T(8,128)(2,1)S(1)}, bf16[512,512]{1,0:T(8,128)(2,1)}, u32[]{:S(2)}) copy-start(bf16[512,512]{1,0:T(8,128)(2,1)} %param.121) | copy-start | bytes 1572868
  0.7 15.3 %copy-start.2 = (bf16[512,512]{1,0:T(8,128)(2,1)S(1)}, bf16[512,512]{1,0:T(8,128)(2,1)}, u32[]{:S(2)}) copy-start(bf16[512,512]{1,0:T(8,128)(2,1)} %param.122) | copy-start | bytes 1572868
  0.7 15.3 %copy-start.3 = (bf16[2,4,512]{2,1,0:T(4,128)(2,1)S(1)}, bf16[2,4,512]{2,1,0:T(4,128)(2,1)}, u32[]{:S(2)}) copy-start(bf16[2,4,512]{2,1,0:T(4,128)(2,1)} %qd_ref.1) | copy-start | bytes 24580
  0.7 15.3 %copy-start.4 = (bf16[2,4,512]{2,1,0:T(4,128)(2,1)S(1)}, bf16[2,4,512]{2,1,0:T(4,128)(2,1)}, u32[]{:S(2)}) copy-start(bf16[2,4,512]{2,1,0:T(4,128)(2,1)} %param.124) | copy-start | bytes 24580
  0.7 15.3 %copy-start.5 = (bf16[2,4,512]{2,1,0:T(4,128)(2,1)S(1)}, bf16[2,4,512]{2,1,0:T(4,128)(2,1)}, u32[]{:S(2)}) copy-start(bf16[2,4,512]{2,1,0:T(4,128)(2,1)} %param.125) | copy-start | bytes 24580
  0.7 15.3 %copy-start.9 = (f32[4]{0:T(128)S(1)}, f32[4]{0:T(128)}, u32[]{:S(2)}) copy-start(f32[4]{0:T(128)} %slopes_ref.1) | copy-start | bytes 52
  4.7 11.3 %collective-permute-start = (bf16[2,4,128,128]{3,2,1,0:T(8,128)(2,1)S(1)}, bf16[2,4,128,128]{3,2,1,0:T(8,128)(2,1)}, u32[]{:S(2)}, u32[]{:S(2)}) collective-permute-start(bf16[2,4,128,128]{3,2,1,0:T(8,128)(2,1)S(1)} %pack.3), channel_id=1, source_target_pairs={{0,384},{8,392},{16,400},{24,408},{32,416},{40,424},{48,432},{56,4... | collective-permute-start | bytes 786440 | tf_op jit(solution)/shard_map/cond/branch_1_fun/ppermute | solution.py:347
  16.0 29.0 %collective-permute-start.13 = (bf16[2,4,128,128]{3,2,1,0:T(8,128)(2,1)}, bf16[2,4,128,128]{3,2,1,0:T(8,128)(2,1)}, u32[]{:S(2)}, u32[]{:S(2)}) collective-permute-start(bf16[2,4,128,128]{3,2,1,0:T(8,128)(2,1)} %get-tuple-element.1363), channel_id=1, source_target_pairs={{0,48},{8,56},{16,32},{24,40},{32,16},{40,24},{48,0},{56,8},{64,11... | collective-permute-start | bytes 786440 | tf_op jit(solution)/shard_map/cond/branch_6_fun/ppermute | solution.py:347
  32.7 5.6 %collective-permute-start.12 = (bf16[4,512,384]{2,1,0:T(8,128)(2,1)}, bf16[4,512,384]{2,1,0:T(8,128)(2,1)}, u32[]{:S(2)}, u32[]{:S(2)}) collective-permute-start(bf16[4,512,384]{2,1,0:T(8,128)(2,1)} %param.21), channel_id=1, source_target_pairs={{0,1},{1,0},{2,3},{3,2},{4,5},{5,4},{6,7},{7,6},{8,9},{9,8},{10,11... | collective-permute-start | bytes 4718600 | tf_op jit(solution)/shard_map/cond/branch_6_fun/cond/branch_1_fun/ppermute | solution.py:341
  47.0 3.8 %collective-permute-start.64 = (bf16[528,512]{1,0:T(8,128)(2,1)S(1)}, bf16[528,512]{1,0:T(8,128)(2,1)S(1)}, u32[]{:S(2)}, u32[]{:S(2)}) collective-permute-start(bf16[528,512]{1,0:T(8,128)(2,1)S(1)} %serve.1.own_ref), channel_id=1, source_target_pairs={{0,1},{1,0},{2,3},{3,2},{4,5},{5,4},{6,7},{7,6},{8,9},{9,8},{10,11... | collective-permute-start | bytes 1622024 | tf_op jit(solution)/shard_map/ppermute | solution.py:400
  52.6 15.0 %collective-permute-start.65 = (bf16[528,384]{1,0:T(8,128)(2,1)S(1)}, bf16[528,384]{1,0:T(8,128)(2,1)S(1)}, u32[]{:S(2)}, u32[]{:S(2)}) collective-permute-start(bf16[528,384]{1,0:T(8,128)(2,1)S(1)} %join0.1), channel_id=1, source_target_pairs={{0,4},{1,5},{2,6},{3,7},{4,0},{5,1},{6,2},{7,3},{8,12},{9,13},{10,... | collective-permute-start | bytes 1216520 | tf_op jit(solution)/shard_map/ppermute | solution.py:403
  58.8 14.8 %collective-permute-start.66 = (bf16[528,384]{1,0:T(8,128)(2,1)S(1)}, bf16[528,384]{1,0:T(8,128)(2,1)S(1)}, u32[]{:S(2)}, u32[]{:S(2)}) collective-permute-start(bf16[528,384]{1,0:T(8,128)(2,1)S(1)} %get-tuple-element.1929), channel_id=1, source_target_pairs={{0,2},{1,3},{2,4},{3,5},{4,6},{5,7},{6,0},{7,1},{8,10},{9,11},{10,... | collective-permute-start | bytes 1216520 | tf_op jit(solution)/shard_map/ppermute | solution.py:403
  62.9 14.0 %collective-permute-start.67 = (bf16[528,384]{1,0:T(8,128)(2,1)S(1)}, bf16[528,384]{1,0:T(8,128)(2,1)S(1)}, u32[]{:S(2)}, u32[]{:S(2)}) collective-permute-start(bf16[528,384]{1,0:T(8,128)(2,1)S(1)} %get-tuple-element.1930), channel_id=1, source_target_pairs={{0,6},{1,7},{2,0},{3,1},{4,2},{5,3},{6,4},{7,5},{8,14},{9,15},{10,... | collective-permute-start | bytes 1216520 | tf_op jit(solution)/shard_map/ppermute | solution.py:403
where the time goes:
time: 78.3 us; the launch traced here: 77.8 us
  waiting for transfers between devices  30.9 us (39%)
  starting transfers between devices  24 us (31%)
  Pallas kernels  19.8 us (25%)
  between operations  2.9 us (4%)
    ppermute x2, waiting for transfers between devices, exchange(): lax.ppermute(array, 'replica', [(i, i ^ pattern) for i in range(size)])  13.3 us
    ppermute x3, waiting for transfers between devices, along(): lax.ppermute(part, 'head', [(i, (i + 2 * away) % devices) for i in range(...  12 us
    ppermute x2, starting transfers between devices, exchange(): lax.ppermute(array, 'replica', [(i, i ^ pattern) for i in range(size)])  11.1 us
    pallas_call x1, Pallas kernels, own_part(): pl.pallas_call(own_kernel, out_shape=(jax.ShapeDtypeStruct((tokens, width...  10.2 us
    ppermute x3, starting transfers between devices, along(): lax.ppermute(part, 'head', [(i, (i + 2 * away) % devices) for i in range(...  9.15 us
    pallas_call x2, Pallas kernels, join(): pl.pallas_call(join_kernel, out_shape=(jax.ShapeDtypeStruct(shape, jnp.bf...  4.8 us
    ppermute x1, waiting for transfers between devices, swapped(): lax.ppermute(own, 'head', siblings())  3.72 us
    pallas_call x1, Pallas kernels, serve(): pl.pallas_call(serve_kernel, out_shape=jax.ShapeDtypeStruct((tokens + PAD...  1.99 us
  transfers between devices with their start and end apart: 7, of which 7 were waited for; matrix products, arithmetic and copies ran while one was open for 0% of the time, Pallas kernels for 17%

commit v1 on v0

--- a/solution.py
+++ b/solution.py
@@ -208,8 +208,9 @@
 
 def serve_kernel(
     place_ref, partner_ref, ids_ref, count_ref, slot_ref, len_ref, decode_ref, slopes_ref,
-    payload_ref, att_ref, dec_ref, q_ref, qd_ref, normed_ref,
+    payload_ref, att_ref, dec_ref, q_ref, qd_ref, theirs_ref, normed_ref, first_ref,
 ):
+    first_ref[...] = theirs_ref[...]
     tokens, width = q_ref.shape
     mate = partner_ref[place_ref[0]]
     prefill_slot = slot_ref[0]
@@ -254,18 +255,23 @@
         normed_ref[tokens:, here] = decoded.astype(jnp.bfloat16)
 
 
-def serve(place, scalars, payload, attended, decoded, q_prefill, q_decode):
+def serve(place, scalars, payload, attended, decoded, q_prefill, q_decode, theirs):
     tokens, width = q_prefill.shape
     scalar = pl.BlockSpec(memory_space=pltpu.SMEM)
     whole = pl.BlockSpec(memory_space=pltpu.VMEM)
+    first = pl.BlockSpec((1, *theirs.shape[1:]), lambda i: (0, 0, 0))
     return pl.pallas_call(
         serve_kernel,
-        out_shape=jax.ShapeDtypeStruct((tokens + PAD, width), jnp.bfloat16),
-        in_specs=[scalar] * 8 + [whole] * 5,
-        out_specs=whole,
-        compiler_params=params(0),
+        out_shape=(
+            jax.ShapeDtypeStruct((tokens + PAD, width), jnp.bfloat16),
+            jax.ShapeDtypeStruct((1, *theirs.shape[1:]), theirs.dtype),
+        ),
+        grid=(1,),
+        in_specs=[scalar] * 8 + [whole] * 5 + [first],
+        out_specs=(whole, first),
+        compiler_params=params(),
         name="serve",
-    )(place, *scalars, payload, attended, decoded, q_prefill, q_decode)
+    )(place, *scalars, payload, attended, decoded, q_prefill, q_decode, theirs)
 
 
 def join_kernel(own_ref, other_ref, *refs):
@@ -396,13 +402,15 @@
         (q_decode, k_decode, v_decode),
         w_out,
     )
-    normed = serve(place, scalars, payload, attended, decoded, q_prefill, q_decode)
+    normed, first = serve(
+        place, scalars, payload, attended, decoded, q_prefill, q_decode, theirs
+    )
     other = lax.ppermute(normed, "head", siblings())
 
     def along(part, away):
         return lax.ppermute(part, "head", [(i, (i + 2 * away) % devices) for i in range(devices)])
 
-    (farthest,) = join(normed, other, mine, theirs, (0,))
+    (farthest,) = join(normed, other, mine, first, (0,))
     farthest, normed = lax.optimization_barrier((farthest, normed))
     *near, here = join(normed, other, mine, theirs, (1, 2, 3))
     near = [along(part, away) for part, away in zip(near, ORDER[1:-1], strict=True)]

time: 78.3 us -> 61.1 us (0.78)
  the two profiles are of different devices: /device:TPU:88 before, /device:TPU:1 now
where the time goes in v1:
time: 61.1 us; the launch traced here: 60.7 us
  starting transfers between devices  21.4 us (35%)
  Pallas kernels  19.5 us (32%)
  waiting for transfers between devices  16.7 us (27%)
  between operations  2.9 us (5%)
    ppermute x3, waiting for transfers between devices, along(): lax.ppermute(part, 'head', [(i, (i + 2 * away) % devices) for i in range(...  11.8 us
    pallas_call x1, Pallas kernels, own_part(): pl.pallas_call(own_kernel, out_shape=(jax.ShapeDtypeStruct((tokens, width...  10.2 us
    ppermute x3, starting transfers between devices, along(): lax.ppermute(part, 'head', [(i, (i + 2 * away) % devices) for i in range(...  8.41 us
    ppermute x1, starting transfers between devices, swapped(): lax.ppermute(own, 'head', siblings())  6.32 us
    ppermute x1, starting transfers between devices, exchange(): lax.ppermute(array, 'replica', [(i, i ^ pattern) for i in range(size)])  4.38 us
    pallas_call x2, Pallas kernels, join(): pl.pallas_call(join_kernel, out_shape=(jax.ShapeDtypeStruct(shape, jnp.bf...  3.81 us
    ppermute x1, waiting for transfers between devices, swapped(): lax.ppermute(own, 'head', siblings())  3.36 us
    pallas_call x1, Pallas kernels, pack(): pl.pallas_call(pack_kernel, out_shape=jax.ShapeDtypeStruct((count, heads,...  2.41 us
  transfers between devices with their start and end apart: 6, of which 4 were waited for; matrix products, arithmetic and copies ran while one was open for 0% of the time, Pallas kernels for 22%

profile of v1, /device:TPU:1, one launch (start us, length us, event | category | flops | bytes accessed | tf_op | source)
XLA Modules:
  0.0 60.7 jit_solution(15727275680492971093)
XLA Ops:
  0.6 0.0 copy-start.6
  0.6 0.0 copy-start.7
  0.7 0.0 copy-start.8
  0.7 0.0 copy-start
  0.7 0.0 copy-start.1
  0.7 0.0 copy-start.2
  0.7 0.0 copy-start.3
  0.7 0.0 copy-start.4
  0.7 0.0 copy-start.5
  0.7 0.0 copy-start.9
  2.8 0.1 pad_add_fusion.place_ref
  2.9 2.4 %conditional.34 = (bf16[2,4,128,128]{3,2,1,0:T(8,128)(2,1)}) conditional(s32[]{:T(128)} %convert_element_type.195, (s32[2]{0:T(128)S(1)}, s32[2,64]{1,0:T(2,128)}, f32[4,4,128,128]{3,2,1,0:T(8,128)}) %tuple.627, (s32[2]{0:T(128)S(1)}, s32[2,64]{1,0:T(2,128)}, f32[4,4,128,128]{3,2,1,0:T(8,128)}) %tuple.628), branch_computations={%region_0.1_spmd, %region_1.2_spmd} | conditional | bytes 1048624 | solution.py:387
  2.9 2.4 %pack.2 = bf16[2,4,128,128]{3,2,1,0:T(8,128)(2,1)} custom-call(s32[2]{0:T(128)S(1)} %get-tuple-element.1213.own_ref, s32[2,64]{1,0:T(2,128)} %get-tuple-element.1232.ids_ref, f32[4,4,128,128]{3,2,1,0:T(8,128)} %get-tuple-element.1233.states_ref), custom_call_target="tpu_custom_call" | custom-call | tf_op jit(solution)/shard_map/cond/branch_0_fun/pack/pallas_call | solution.py:44
  5.3 0.0 copy-done.6
  5.3 0.0 copy-done.7
  5.3 0.0 copy-done.8
  5.3 0.0 copy-done
  5.3 0.0 copy-done.1
  5.3 0.0 copy-done.2
  5.3 0.0 copy-done.3
  5.3 0.0 copy-done.4
  5.3 0.0 copy-done.5
  5.4 0.0 copy-done.9
  5.4 24.4 %conditional.35 = (bf16[2,4,128,128]{3,2,1,0:T(8,128)(2,1)}, f32[512,512]{1,0:T(8,128)}, f32[8,512]{1,0:T(8,128)S(1)}, bf16[4,512,384]{2,1,0:T(8,128)(2,1)S(1)}, bf16[4,512,384]{2,1,0:T(8,128)(2,1)}) conditional(s32[]{:T(128)} %clamp.3, (bf16[2,4,128,128]{3,2,1,0:T(8,128)(2,1)}, s32[2]{0:T(128)S(1)}, ...), branch_computations={%region_2.5_spmd, %region_5.8_spmd, %region_8.11_spmd, %region_11.... | conditional | flops 335544320 | bytes 16253070 | solution.py:394
  5.4 4.4 %collective-permute-start.3 = (bf16[2,4,128,128]{3,2,1,0:T(8,128)(2,1)}, bf16[2,4,128,128]{3,2,1,0:T(8,128)(2,1)}, u32[]{:S(2)}, u32[]{:S(2)}) collective-permute-start(bf16[2,4,128,128]{3,2,1,0:T(8,128)(2,1)} %get-tuple-element.1258), channel_id=1, source_target_pairs={{0,8},{8,0},{16,24},{24,16},{32,40},{40,32},{48,56},{56,48},{64,72... | collective-permute-start | bytes 786440 | tf_op jit(solution)/shard_map/cond/branch_1_fun/ppermute | solution.py:353
  9.8 10.2 %own_part.33 = (f32[512,512]{1,0:T(8,128)}, f32[8,512]{1,0:T(8,128)S(1)}, bf16[4,512,384]{2,1,0:T(8,128)(2,1)S(1)}, bf16[4,512,384]{2,1,0:T(8,128)(2,1)}) custom-call(s32[2]{0:T(128)S(1)} %get-tuple-element.1259.place_ref, s32[64]{0:T(128)S(1)} %get-tuple-element.1260.partner_ref, s32[2,64]{1,0:T(2,128)} %get-tuple-element.1261.ids_ref, ...), custom_call_target="tpu_custom_call" | custom-call | flops 335544320 | bytes 8912896 | tf_op jit(solution)/shard_map/cond/branch_1_fun/own_part/pallas_call | solution.py:169
  20.0 9.7 %conditional.1 = (bf16[4,512,384]{2,1,0:T(8,128)(2,1)}) conditional(s32[]{:T(128)} %bitcast.1, () %tuple.236, bf16[4,512,384]{2,1,0:T(8,128)(2,1)} %get-tuple-element.1278), branch_computations={%region_6.6_spmd, %region_7.7_spmd} | conditional | bytes 6291504 | solution.py:346
  20.0 6.3 %collective-permute-start.2 = (bf16[4,512,384]{2,1,0:T(8,128)(2,1)}, bf16[4,512,384]{2,1,0:T(8,128)(2,1)}, u32[]{:S(2)}, u32[]{:S(2)}) collective-permute-start(bf16[4,512,384]{2,1,0:T(8,128)(2,1)} %param.6), channel_id=1, source_target_pairs={{0,1},{1,0},{2,3},{3,2},{4,5},{5,4},{6,7},{7,6},{8,9},{9,8},{10,11... | collective-permute-start | bytes 4718600 | tf_op jit(solution)/shard_map/cond/branch_1_fun/cond/branch_1_fun/ppermute | solution.py:347
  26.4 3.4 %collective-permute-done.2 = bf16[4,512,384]{2,1,0:T(8,128)(2,1)} collective-permute-done((bf16[4,512,384]{2,1,0:T(8,128)(2,1)}, bf16[4,512,384]{2,1,0:T(8,128)(2,1)}, u32[]{:S(2)}, u32[]{:S(2)}) %collective-permute-start.2) | collective-permute-done | bytes 1572896 | tf_op jit(solution)/shard_map/cond/branch_1_fun/cond/branch_1_fun/ppermute | solution.py:347
  29.7 0.0 collective-permute-done.3
  29.7 2.1 %serve.1 = (bf16[528,512]{1,0:T(8,128)(2,1)S(1)}, bf16[1,512,384]{2,1,0:T(8,128)(2,1)S(1)}) custom-call(s32[2]{0:T(128)S(1)} %pad_add_fusion.place_ref, s32[64]{0:T(128)S(1)} %copy-done.6, s32[2,64]{1,0:T(2,128)} %bitcast.103, s32[64]{0:T(128)S(1)} %copy-done.7, s32[1]{0:T(128)S(6)} %copy.243.slot_ref, s32[1]{0:T(128)S(6)} %copy.244.len_ref, ...), custom_call_target="tpu_custom_call" | custom-call | tf_op jit(solution)/shard_map/serve/pallas_call | solution.py:263
  31.8 2.3 %collective-permute-start.64 = (bf16[528,512]{1,0:T(8,128)(2,1)S(1)}, bf16[528,512]{1,0:T(8,128)(2,1)S(1)}, u32[]{:S(2)}, u32[]{:S(2)}) collective-permute-start(bf16[528,512]{1,0:T(8,128)(2,1)S(1)} %get-tuple-element.1931.own_ref), channel_id=1, source_target_pairs={{0,1},{1,0},{2,3},{3,2},{4,5},{5,4},{6,7},{7,6},{8,9},{9,8},{10,11... | collective-permute-start | bytes 1622024 | tf_op jit(solution)/shard_map/ppermute | solution.py:408
  34.1 1.5 %collective-permute-done.64.other_ref = bf16[528,512]{1,0:T(8,128)(2,1)S(1)} collective-permute-done((bf16[528,512]{1,0:T(8,128)(2,1)S(1)}, bf16[528,512]{1,0:T(8,128)(2,1)S(1)}, u32[]{:S(2)}, u32[]{:S(2)}) %collective-permute-start.64) | collective-permute-done | bytes 540704 | tf_op jit(solution)/shard_map/ppermute | solution.py:408
  35.7 0.7 %join0.1 = bf16[528,384]{1,0:T(8,128)(2,1)S(1)} custom-call(bf16[528,512]{1,0:T(8,128)(2,1)S(1)} %get-tuple-element.1931.own_ref, bf16[528,512]{1,0:T(8,128)(2,1)S(1)} %collective-permute-done.64.other_ref, bf16[4,512,384]{2,1,0:T(8,128)(2,1)S(1)} %get-tuple-element.1928.refs_0_.refs_1_.refs_2_, bf16[1,512,384]{2,1,0:T(8,128)(2,1)S(1)} %get-tuple-element.1929.refs_1_), custom_call_target="tpu_custom_call" | custom-call | flops 415236096 | bytes 1867776 | tf_op jit(solution)/shard_map/join0/pallas_call | solution.py:289
  36.4 1.9 %collective-permute-start.65 = (bf16[528,384]{1,0:T(8,128)(2,1)S(1)}, bf16[528,384]{1,0:T(8,128)(2,1)S(1)}, u32[]{:S(2)}, u32[]{:S(2)}) collective-permute-start(bf16[528,384]{1,0:T(8,128)(2,1)S(1)} %join0.1), channel_id=1, source_target_pairs={{0,4},{1,5},{2,6},{3,7},{4,0},{5,1},{6,2},{7,3},{8,12},{9,13},{10,... | collective-permute-start | bytes 1216520 | tf_op jit(solution)/shard_map/ppermute | solution.py:411
  38.3 3.1 %join1.1 = (bf16[528,384]{1,0:T(8,128)(2,1)S(1)}, bf16[528,384]{1,0:T(8,128)(2,1)S(1)}, bf16[528,384]{1,0:T(8,128)(2,1)S(1)}) custom-call(bf16[528,512]{1,0:T(8,128)(2,1)S(1)} %get-tuple-element.1931.own_ref, bf16[528,512]{1,0:T(8,128)(2,1)S(1)} %collective-permute-done.64.other_ref, bf16[4,512,384]{2,1,0:T(8,128)(2,1)S(1)} %get-tuple-element.1928.refs_0_.refs_1_.refs_2_, ...), custom_call_target="tpu_custom_call" | custom-call | flops 1245708288 | bytes 3440640 | tf_op jit(solution)/shard_map/join1/pallas_call | solution.py:289
  41.4 1.9 %collective-permute-start.66 = (bf16[528,384]{1,0:T(8,128)(2,1)S(1)}, bf16[528,384]{1,0:T(8,128)(2,1)S(1)}, u32[]{:S(2)}, u32[]{:S(2)}) collective-permute-start(bf16[528,384]{1,0:T(8,128)(2,1)S(1)} %get-tuple-element.1933), channel_id=1, source_target_pairs={{0,2},{1,3},{2,4},{3,5},{4,6},{5,7},{6,0},{7,1},{8,10},{9,11},{10,... | collective-permute-start | bytes 1216520 | tf_op jit(solution)/shard_map/ppermute | solution.py:411
  43.3 4.6 %collective-permute-start.67 = (bf16[528,384]{1,0:T(8,128)(2,1)S(1)}, bf16[528,384]{1,0:T(8,128)(2,1)S(1)}, u32[]{:S(2)}, u32[]{:S(2)}) collective-permute-start(bf16[528,384]{1,0:T(8,128)(2,1)S(1)} %get-tuple-element.1934), channel_id=1, source_target_pairs={{0,6},{1,7},{2,0},{3,1},{4,2},{5,3},{6,4},{7,5},{8,14},{9,15},{10,... | collective-permute-start | bytes 1216520 | tf_op jit(solution)/shard_map/ppermute | solution.py:411
  47.9 2.5 %collective-permute-done.65.a_ref = bf16[528,384]{1,0:T(8,128)(2,1)S(1)} collective-permute-done((bf16[528,384]{1,0:T(8,128)(2,1)S(1)}, bf16[528,384]{1,0:T(8,128)(2,1)S(1)}, u32[]{:S(2)}, u32[]{:S(2)}) %collective-permute-start.65) | collective-permute-done | bytes 405536 | tf_op jit(solution)/shard_map/ppermute | solution.py:411
  50.4 0.1 add.3.a_ref
  50.5 9.3 %collective-permute-done.66.b_ref = bf16[528,384]{1,0:T(8,128)(2,1)S(1)} collective-permute-done((bf16[528,384]{1,0:T(8,128)(2,1)S(1)}, bf16[528,384]{1,0:T(8,128)(2,1)S(1)}, u32[]{:S(2)}, u32[]{:S(2)}) %collective-permute-start.66) | collective-permute-done | bytes 405536 | tf_op jit(solution)/shard_map/ppermute | solution.py:411
  59.8 0.0 collective-permute-done.67.c_ref
  59.8 0.9 %finish.1 = (bf16[512,384]{1,0:T(8,128)(2,1)}, bf16[2,4,384]{2,1,0:T(4,128)(2,1)}) custom-call(f32[528,384]{1,0:T(8,128)S(1)} %add.3.a_ref, bf16[528,384]{1,0:T(8,128)(2,1)S(1)} %collective-permute-done.66.b_ref, bf16[528,384]{1,0:T(8,128)(2,1)S(1)} %collective-permute-done.67.c_ref), custom_call_target="tpu_custom_call" | custom-call | tf_op jit(solution)/shard_map/finish/pallas_call | solution.py:330
Async XLA Ops:
  0.6 4.7 %copy-start.6 = (s32[64]{0:T(128)S(1)}, s32[64]{0:T(128)}, u32[]{:S(2)}) copy-start(s32[64]{0:T(128)} %partner_ref.1) | copy-start | bytes 772
  0.6 4.6 %copy-start.7 = (s32[64]{0:T(128)S(1)}, s32[64]{0:T(128)}, u32[]{:S(2)}) copy-start(s32[64]{0:T(128)} %count_ref.1) | copy-start | bytes 772
  0.7 4.6 %copy-start.8 = (s32[1,4]{1,0:T(1,128)S(1)}, s32[1,4]{1,0:T(1,128)}, u32[]{:S(2)}) copy-start(s32[1,4]{1,0:T(1,128)} %decode_ref.1) | copy-start | bytes 52
  0.7 4.6 %copy-start = (bf16[512,512]{1,0:T(8,128)(2,1)S(1)}, bf16[512,512]{1,0:T(8,128)(2,1)}, u32[]{:S(2)}) copy-start(bf16[512,512]{1,0:T(8,128)(2,1)} %q_ref.1) | copy-start | bytes 1572868
  0.7 4.6 %copy-start.1 = (bf16[512,512]{1,0:T(8,128)(2,1)S(1)}, bf16[512,512]{1,0:T(8,128)(2,1)}, u32[]{:S(2)}) copy-start(bf16[512,512]{1,0:T(8,128)(2,1)} %param.121) | copy-start | bytes 1572868
  0.7 4.6 %copy-start.2 = (bf16[512,512]{1,0:T(8,128)(2,1)S(1)}, bf16[512,512]{1,0:T(8,128)(2,1)}, u32[]{:S(2)}) copy-start(bf16[512,512]{1,0:T(8,128)(2,1)} %param.122) | copy-start | bytes 1572868
  0.7 4.6 %copy-start.3 = (bf16[2,4,512]{2,1,0:T(4,128)(2,1)S(1)}, bf16[2,4,512]{2,1,0:T(4,128)(2,1)}, u32[]{:S(2)}) copy-start(bf16[2,4,512]{2,1,0:T(4,128)(2,1)} %qd_ref.1) | copy-start | bytes 24580
  0.7 4.6 %copy-start.4 = (bf16[2,4,512]{2,1,0:T(4,128)(2,1)S(1)}, bf16[2,4,512]{2,1,0:T(4,128)(2,1)}, u32[]{:S(2)}) copy-start(bf16[2,4,512]{2,1,0:T(4,128)(2,1)} %param.124) | copy-start | bytes 24580
  0.7 4.6 %copy-start.5 = (bf16[2,4,512]{2,1,0:T(4,128)(2,1)S(1)}, bf16[2,4,512]{2,1,0:T(4,128)(2,1)}, u32[]{:S(2)}) copy-start(bf16[2,4,512]{2,1,0:T(4,128)(2,1)} %param.125) | copy-start | bytes 24580
  0.7 4.6 %copy-start.9 = (f32[4]{0:T(128)S(1)}, f32[4]{0:T(128)}, u32[]{:S(2)}) copy-start(f32[4]{0:T(128)} %slopes_ref.1) | copy-start | bytes 52
  5.4 24.3 %collective-permute-start.3 = (bf16[2,4,128,128]{3,2,1,0:T(8,128)(2,1)}, bf16[2,4,128,128]{3,2,1,0:T(8,128)(2,1)}, u32[]{:S(2)}, u32[]{:S(2)}) collective-permute-start(bf16[2,4,128,128]{3,2,1,0:T(8,128)(2,1)} %get-tuple-element.1258), channel_id=1, source_target_pairs={{0,8},{8,0},{16,24},{24,16},{32,40},{40,32},{48,56},{56,48},{64,72... | collective-permute-start | bytes 786440 | tf_op jit(solution)/shard_map/cond/branch_1_fun/ppermute | solution.py:353
  20.0 9.7 %collective-permute-start.2 = (bf16[4,512,384]{2,1,0:T(8,128)(2,1)}, bf16[4,512,384]{2,1,0:T(8,128)(2,1)}, u32[]{:S(2)}, u32[]{:S(2)}) collective-permute-start(bf16[4,512,384]{2,1,0:T(8,128)(2,1)} %param.6), channel_id=1, source_target_pairs={{0,1},{1,0},{2,3},{3,2},{4,5},{5,4},{6,7},{7,6},{8,9},{9,8},{10,11... | collective-permute-start | bytes 4718600 | tf_op jit(solution)/shard_map/cond/branch_1_fun/cond/branch_1_fun/ppermute | solution.py:347
  31.8 3.8 %collective-permute-start.64 = (bf16[528,512]{1,0:T(8,128)(2,1)S(1)}, bf16[528,512]{1,0:T(8,128)(2,1)S(1)}, u32[]{:S(2)}, u32[]{:S(2)}) collective-permute-start(bf16[528,512]{1,0:T(8,128)(2,1)S(1)} %get-tuple-element.1931.own_ref), channel_id=1, source_target_pairs={{0,1},{1,0},{2,3},{3,2},{4,5},{5,4},{6,7},{7,6},{8,9},{9,8},{10,11... | collective-permute-start | bytes 1622024 | tf_op jit(solution)/shard_map/ppermute | solution.py:408
  36.4 14.0 %collective-permute-start.65 = (bf16[528,384]{1,0:T(8,128)(2,1)S(1)}, bf16[528,384]{1,0:T(8,128)(2,1)S(1)}, u32[]{:S(2)}, u32[]{:S(2)}) collective-permute-start(bf16[528,384]{1,0:T(8,128)(2,1)S(1)} %join0.1), channel_id=1, source_target_pairs={{0,4},{1,5},{2,6},{3,7},{4,0},{5,1},{6,2},{7,3},{8,12},{9,13},{10,... | collective-permute-start | bytes 1216520 | tf_op jit(solution)/shard_map/ppermute | solution.py:411
  41.4 18.4 %collective-permute-start.66 = (bf16[528,384]{1,0:T(8,128)(2,1)S(1)}, bf16[528,384]{1,0:T(8,128)(2,1)S(1)}, u32[]{:S(2)}, u32[]{:S(2)}) collective-permute-start(bf16[528,384]{1,0:T(8,128)(2,1)S(1)} %get-tuple-element.1933), channel_id=1, source_target_pairs={{0,2},{1,3},{2,4},{3,5},{4,6},{5,7},{6,0},{7,1},{8,10},{9,11},{10,... | collective-permute-start | bytes 1216520 | tf_op jit(solution)/shard_map/ppermute | solution.py:411
  43.3 16.5 %collective-permute-start.67 = (bf16[528,384]{1,0:T(8,128)(2,1)S(1)}, bf16[528,384]{1,0:T(8,128)(2,1)S(1)}, u32[]{:S(2)}, u32[]{:S(2)}) collective-permute-start(bf16[528,384]{1,0:T(8,128)(2,1)S(1)} %get-tuple-element.1934), channel_id=1, source_target_pairs={{0,6},{1,7},{2,0},{3,1},{4,2},{5,3},{6,4},{7,5},{8,14},{9,15},{10,... | collective-permute-start | bytes 1216520 | tf_op jit(solution)/shard_map/ppermute | solution.py:411

commit v2 on v1

--- a/solution.py
+++ b/solution.py
@@ -82,11 +82,24 @@
 
 def own_kernel(
     place_ref, partner_ref, ids_ref, count_ref, slot_ref, len_ref, decode_ref, slopes_ref,
-    states_ref, q_ref, k_ref, v_ref, qd_ref, kd_ref, vd_ref, mine_ref, theirs_ref,
-    att_ref, dec_ref, mine_out_ref, theirs_out_ref, mem_ref,
+    states_ref, q_ref, k_ref, v_ref, qd_ref, kd_ref, vd_ref,
+    w_ref, att_ref, dec_ref, mine_out_ref, theirs_out_ref, info_ref, mem_ref, sems,
 ):
-    mine_out_ref[0] = mine_ref[...]
-    theirs_out_ref[0] = theirs_ref[...]
+    info_ref[0] = slot_ref[0]
+    info_ref[1] = len_ref[0]
+    width, cols = mine_out_ref.shape[1:]
+    chip, core = far_chip(place_ref, pl.program_id(0)), lax.rem(place_ref[1], 2)
+    taken = [
+        pltpu.make_async_copy(
+            w_ref.at[:, pl.ds(pl.multiple_of((2 * chip + of) * cols, cols), cols)], out.at[0], sem
+        )
+        for of, out, sem in (
+            (core, mine_out_ref, sems.at[0]),
+            (1 - core, theirs_out_ref, sems.at[1]),
+        )
+    ]
+    for copy in taken:
+        copy.start()
     slope = slopes_ref[pl.program_id(0)]
     own = place_ref[0]
     mate = partner_ref[own]
@@ -141,6 +154,8 @@
     before = product(queries[second], keys[first]) * values[first]
     dec_ref[first, :] = keep * seen[first] + now[first]
     dec_ref[second, :] = keep * (keep * seen[second] + before) + now[second]
+    for copy in taken:
+        copy.wait()
 
 
 def far_chip(place, step):
@@ -159,13 +174,6 @@
     row = pl.BlockSpec((steps, slots, DK), lambda h, *_: (0, 0, h))
     taken = pl.BlockSpec((1, width, cols), lambda h, *_: (h, 0, 0))
 
-    def weights(other):
-        def index(h, place, *_):
-            core = lax.rem(place[1], 2)
-            return (0, 2 * far_chip(place, h) + (1 - core if other else core))
-
-        return pl.BlockSpec((width, cols), index)
-
     return pl.pallas_call(
         own_kernel,
         out_shape=(
@@ -173,6 +181,7 @@
             jax.ShapeDtypeStruct((steps * slots, width), jnp.float32),
             jax.ShapeDtypeStruct((4, width, cols), jnp.bfloat16),
             jax.ShapeDtypeStruct((4, width, cols), jnp.bfloat16),
+            jax.ShapeDtypeStruct((2,), jnp.int32),
         ),
         grid_spec=pltpu.PrefetchScalarGridSpec(
             num_scalar_prefetch=8,
@@ -185,16 +194,16 @@
                 row,
                 row,
                 row,
-                weights(False),
-                weights(True),
+                pl.BlockSpec(memory_space=pl.ANY),
             ],
             out_specs=(
                 column,
                 pl.BlockSpec((steps * slots, DK), lambda h, *_: (0, h)),
                 taken,
                 taken,
+                pl.BlockSpec(memory_space=pltpu.SMEM),
             ),
-            scratch_shapes=[pltpu.VMEM((DK, DK), jnp.float32)],
+            scratch_shapes=[pltpu.VMEM((DK, DK), jnp.float32), pltpu.SemaphoreType.DMA((2,))],
         ),
         compiler_params=params(),
         cost_estimate=pl.CostEstimate(
@@ -203,18 +212,18 @@
             transcendentals=0,
         ),
         name="own_part",
-    )(place, *scalars, states, *prefill, *decode, w_out, w_out)
+    )(place, *scalars, states, *prefill, *decode, w_out)
 
 
 def serve_kernel(
-    place_ref, partner_ref, ids_ref, count_ref, slot_ref, len_ref, decode_ref, slopes_ref,
+    place_ref, partner_ref, ids_ref, count_ref, info_ref, decode_ref, slopes_ref,
     payload_ref, att_ref, dec_ref, q_ref, qd_ref, theirs_ref, normed_ref, first_ref,
 ):
     first_ref[...] = theirs_ref[...]
     tokens, width = q_ref.shape
     mate = partner_ref[place_ref[0]]
-    prefill_slot = slot_ref[0]
-    length = len_ref[0]
+    prefill_slot = info_ref[0]
+    length = info_ref[1]
     slots = decode_ref.shape[1]
     entries = ids_ref.shape[0]
     lands = [
@@ -267,7 +276,7 @@
             jax.ShapeDtypeStruct((1, *theirs.shape[1:]), theirs.dtype),
         ),
         grid=(1,),
-        in_specs=[scalar] * 8 + [whole] * 5 + [first],
+        in_specs=[scalar] * 7 + [whole] * 5 + [first],
         out_specs=(whole, first),
         compiler_params=params(),
         name="serve",
@@ -388,10 +397,10 @@
 
     def branch(rest, payload, *arrays):
         moving = exchange(payload, rest) if rest else copied(payload)
-        attended, decoded, mine, theirs = own_part(*arrays)
-        return moving, attended, decoded, mine, swapped(partner, theirs)
-
-    payload, attended, decoded, mine, theirs = lax.switch(
+        attended, decoded, mine, theirs, info = own_part(*arrays)
+        return moving, attended, decoded, mine, swapped(partner, theirs), info
+
+    payload, attended, decoded, mine, theirs, info = lax.switch(
         jnp.where(pattern >= half, pattern ^ across, pattern),
         [partial(branch, rest) for rest in range(half)],
         payload,
@@ -402,6 +411,7 @@
         (q_decode, k_decode, v_decode),
         w_out,
     )
+    scalars = (partner, ids, send_count, info, decode_slots, slopes)
     normed, first = serve(
         place, scalars, payload, attended, decoded, q_prefill, q_decode, theirs
     )

time: 61.1 us -> 81.9 us (1.34); the launches traced: 60.7 us -> 80.4 us
  starting transfers between devices: 21.4 us -> 36.2 us
  waiting for transfers between devices: 16.7 us -> 23.7 us
  between operations: 2.9 us -> 1.61 us
  Pallas kernels: 19.5 us -> 18.5 us
    ppermute x1 -> x2, starting transfers between devices: 4.38 us -> 18.2 us  [exchange(): lax.ppermute(array, 'replica', [(i, i ^ pattern) for i in range(size)])]
    ppermute x1 -> x2, waiting for transfers between devices: 0.01 us -> 10.2 us  [exchange(): lax.ppermute(array, 'replica', [(i, i ^ pattern) for i in range(size)])]
    ppermute x3, waiting for transfers between devices: 11.8 us -> 8.52 us  [along(): lax.ppermute(part, 'head', [(i, (i + 2 * away) % devices) for i in range(...]
    ppermute x3, starting transfers between devices: 8.41 us -> 11.3 us  [along(): lax.ppermute(part, 'head', [(i, (i + 2 * away) % devices) for i in range(...]
    ppermute x1, starting transfers between devices: 6.32 us -> 3.74 us  [swapped(): lax.ppermute(own, 'head', siblings())]
  transfers between devices with their start and end apart: 6 -> 7, of which waited for: 4 -> 5; matrix products, arithmetic and copies ran while one was open for 0% -> 0% of each run, Pallas kernels for 22% -> 16%
where the time goes in v2:
time: 81.9 us; the launch traced here: 80.4 us
  starting transfers between devices  36.2 us (44%)
  waiting for transfers between devices  23.7 us (29%)
  Pallas kernels  18.5 us (23%)
  between operations  1.61 us (2%)
    ppermute x2, starting transfers between devices, exchange(): lax.ppermute(array, 'replica', [(i, i ^ pattern) for i in range(size)])  18.2 us
    ppermute x3, starting transfers between devices, along(): lax.ppermute(part, 'head', [(i, (i + 2 * away) % devices) for i in range(...  11.3 us
    ppermute x2, waiting for transfers between devices, exchange(): lax.ppermute(array, 'replica', [(i, i ^ pattern) for i in range(size)])  10.2 us
    pallas_call x1, Pallas kernels, own_part(): pl.pallas_call(own_kernel, out_shape=(jax.ShapeDtypeStruct((tokens, width...  9.85 us
    ppermute x3, waiting for transfers between devices, along(): lax.ppermute(part, 'head', [(i, (i + 2 * away) % devices) for i in range(...  8.52 us
    pallas_call x2, Pallas kernels, join(): pl.pallas_call(join_kernel, out_shape=(jax.ShapeDtypeStruct(shape, jnp.bf...  3.8 us
    ppermute x1, starting transfers between devices, swapped(): lax.ppermute(own, 'head', siblings())  3.74 us
    ppermute x1, waiting for transfers between devices, swapped(): lax.ppermute(own, 'head', siblings())  3.36 us
  transfers between devices with their start and end apart: 7, of which 5 were waited for; matrix products, arithmetic and copies ran while one was open for 0% of the time, Pallas kernels for 16%

profile of v2, /device:TPU:1, one launch (start us, length us, event | category | flops | bytes accessed | tf_op | source)
XLA Modules:
  0.0 80.4 jit_solution(15728063338093853763)
XLA Ops:
  0.6 0.0 copy-start.6
  0.6 0.0 copy-start.9
  0.7 0.0 copy-start.3
  0.7 0.0 copy-start
  0.7 0.0 copy-start.8
  0.7 0.0 copy-start.7
  0.7 0.0 copy-start.5
  0.7 0.0 copy-start.4
  0.7 0.0 copy-start.2
  0.7 0.0 copy-start.1
  1.5 0.1 pad_add_fusion.place_ref
  1.6 10.9 %conditional.34 = (bf16[2,4,128,128]{3,2,1,0:T(8,128)(2,1)}) conditional(s32[]{:T(128)} %convert_element_type.195, (s32[2]{0:T(128)S(1)}, s32[2,64]{1,0:T(2,128)}, f32[4,4,128,128]{3,2,1,0:T(8,128)}) %tuple.627, (s32[2]{0:T(128)S(1)}, s32[2,64]{1,0:T(2,128)}, f32[4,4,128,128]{3,2,1,0:T(8,128)}) %tuple.628), branch_computations={%region_0.1_spmd, %region_1.2_spmd} | conditional | bytes 1048624 | solution.py:396
  1.6 1.8 %pack.3 = bf16[2,4,128,128]{3,2,1,0:T(8,128)(2,1)S(1)} custom-call(s32[2]{0:T(128)S(1)} %get-tuple-element.1234.own_ref, s32[2,64]{1,0:T(2,128)} %get-tuple-element.1235.ids_ref, f32[4,4,128,128]{3,2,1,0:T(8,128)} %get-tuple-element.1236.states_ref), custom_call_target="tpu_custom_call" | custom-call | tf_op jit(solution)/shard_map/cond/branch_1_fun/pack/pallas_call | solution.py:44
  3.4 5.2 %collective-permute-start = (bf16[2,4,128,128]{3,2,1,0:T(8,128)(2,1)S(1)}, bf16[2,4,128,128]{3,2,1,0:T(8,128)(2,1)}, u32[]{:S(2)}, u32[]{:S(2)}) collective-permute-start(bf16[2,4,128,128]{3,2,1,0:T(8,128)(2,1)S(1)} %pack.3), channel_id=1, source_target_pairs={{0,384},{8,392},{16,400},{24,408},{32,416},{40,424},{48,432},{56,4... | collective-permute-start | bytes 786440 | tf_op jit(solution)/shard_map/cond/branch_1_fun/ppermute | solution.py:362
  8.6 3.9 %collective-permute-done = bf16[2,4,128,128]{3,2,1,0:T(8,128)(2,1)} collective-permute-done((bf16[2,4,128,128]{3,2,1,0:T(8,128)(2,1)S(1)}, bf16[2,4,128,128]{3,2,1,0:T(8,128)(2,1)}, u32[]{:S(2)}, u32[]{:S(2)}) %collective-permute-start) | collective-permute-done | bytes 262176 | tf_op jit(solution)/shard_map/cond/branch_1_fun/ppermute | solution.py:362
  12.4 0.0 copy-done.6
  12.5 0.0 copy-done.9
  12.5 0.0 copy-done.3
  12.5 0.0 copy-done
  12.5 0.0 copy-done.8
  12.5 0.0 copy-done.7
  12.5 0.0 copy-done.5
  12.5 0.0 copy-done.4
  12.5 0.0 copy-done.2
  12.5 0.0 copy-done.1
  12.5 36.6 %conditional.35 = (bf16[2,4,128,128]{3,2,1,0:T(8,128)(2,1)}, f32[512,512]{1,0:T(8,128)}, f32[8,512]{1,0:T(8,128)S(1)}, bf16[4,512,384]{2,1,0:T(8,128)(2,1)S(1)},...) conditional(s32[]{:T(128)} %clamp.3, (bf16[2,4,128,128]{3,2,1,0:T(8,128)(2,1)}, ...), branch_computations={%region_2.5_spmd, %region_5.8_spmd, %region_8.11_spmd, %region_11.... | conditional | flops 335544320 | bytes 16253078 | solution.py:403
  12.8 13.0 %collective-permute-start.63 = (bf16[2,4,128,128]{3,2,1,0:T(8,128)(2,1)}, bf16[2,4,128,128]{3,2,1,0:T(8,128)(2,1)}, u32[]{:S(2)}, u32[]{:S(2)}) collective-permute-start(bf16[2,4,128,128]{3,2,1,0:T(8,128)(2,1)} %get-tuple-element.1919), channel_id=1, source_target_pairs={{0,248},{8,240},{16,232},{24,224},{32,216},{40,208},{48,200},{56,1... | collective-permute-start | bytes 786440 | tf_op jit(solution)/shard_map/cond/branch_31_fun/ppermute | solution.py:362
  25.8 9.9 %own_part.63 = (f32[512,512]{1,0:T(8,128)}, f32[8,512]{1,0:T(8,128)S(1)}, bf16[4,512,384]{2,1,0:T(8,128)(2,1)S(1)}, bf16[4,512,384]{2,1,0:T(8,128)(2,1)}, s32[2]{0:T(128)S(1)}) custom-call(s32[2]{0:T(128)S(1)} %get-tuple-element.1920.place_ref, s32[64]{0:T(128)S(1)} %get-tuple-element.1921.partner_ref, s32[2,64]{1,0:T(2,128)} %get-tuple-element.1922.ids_ref, ...), custom_call_target="tpu_custom_call" | custom-call | flops 335544320 | bytes 8912896 | tf_op jit(solution)/shard_map/cond/branch_31_fun/own_part/pallas_call | solution.py:177
  35.7 7.1 %conditional.31 = (bf16[4,512,384]{2,1,0:T(8,128)(2,1)}) conditional(s32[]{:T(128)} %bitcast.31, () %tuple.296, bf16[4,512,384]{2,1,0:T(8,128)(2,1)} %get-tuple-element.1939), branch_computations={%region_96.96_spmd, %region_97.97_spmd} | conditional | bytes 6291504 | solution.py:355
  35.7 3.7 %collective-permute-start.62 = (bf16[4,512,384]{2,1,0:T(8,128)(2,1)}, bf16[4,512,384]{2,1,0:T(8,128)(2,1)}, u32[]{:S(2)}, u32[]{:S(2)}) collective-permute-start(bf16[4,512,384]{2,1,0:T(8,128)(2,1)} %param.96), channel_id=1, source_target_pairs={{0,1},{1,0},{2,3},{3,2},{4,5},{5,4},{6,7},{7,6},{8,9},{9,8},{10,11... | collective-permute-start | bytes 4718600 | tf_op jit(solution)/shard_map/cond/branch_31_fun/cond/branch_1_fun/ppermute | solution.py:356
  39.4 3.4 %collective-permute-done.62 = bf16[4,512,384]{2,1,0:T(8,128)(2,1)} collective-permute-done((bf16[4,512,384]{2,1,0:T(8,128)(2,1)}, bf16[4,512,384]{2,1,0:T(8,128)(2,1)}, u32[]{:S(2)}, u32[]{:S(2)}) %collective-permute-start.62) | collective-permute-done | bytes 1572896 | tf_op jit(solution)/shard_map/cond/branch_31_fun/cond/branch_1_fun/ppermute | solution.py:356
  42.8 6.4 %collective-permute-done.63 = bf16[2,4,128,128]{3,2,1,0:T(8,128)(2,1)} collective-permute-done((bf16[2,4,128,128]{3,2,1,0:T(8,128)(2,1)}, bf16[2,4,128,128]{3,2,1,0:T(8,128)(2,1)}, u32[]{:S(2)}, u32[]{:S(2)}) %collective-permute-start.63) | collective-permute-done | bytes 262176 | tf_op jit(solution)/shard_map/cond/branch_31_fun/ppermute | solution.py:362
  49.2 2.1 %serve.1 = (bf16[528,512]{1,0:T(8,128)(2,1)S(1)}, bf16[1,512,384]{2,1,0:T(8,128)(2,1)S(1)}) custom-call(s32[2]{0:T(128)S(1)} %pad_add_fusion.place_ref, s32[64]{0:T(128)S(1)} %copy-done.6, s32[2,64]{1,0:T(2,128)} %bitcast.103, s32[64]{0:T(128)S(1)} %copy-done.7, s32[2]{0:T(128)S(1)} %get-tuple-element.1956.info_ref, s32[1,4]{1,0:T(1,128)S(1)} %copy-done.8, ...), custom_call_target="tpu_custom_call" | custom-call | tf_op jit(solution)/shard_map/serve/pallas_call | solution.py:272
  51.3 2.9 %collective-permute-start.64 = (bf16[528,512]{1,0:T(8,128)(2,1)S(1)}, bf16[528,512]{1,0:T(8,128)(2,1)S(1)}, u32[]{:S(2)}, u32[]{:S(2)}) collective-permute-start(bf16[528,512]{1,0:T(8,128)(2,1)S(1)} %get-tuple-element.1965.own_ref), channel_id=1, source_target_pairs={{0,1},{1,0},{2,3},{3,2},{4,5},{5,4},{6,7},{7,6},{8,9},{9,8},{10,11... | collective-permute-start | bytes 1622024 | tf_op jit(solution)/shard_map/ppermute | solution.py:418
  54.2 1.5 %collective-permute-done.64.other_ref = bf16[528,512]{1,0:T(8,128)(2,1)S(1)} collective-permute-done((bf16[528,512]{1,0:T(8,128)(2,1)S(1)}, bf16[528,512]{1,0:T(8,128)(2,1)S(1)}, u32[]{:S(2)}, u32[]{:S(2)}) %collective-permute-start.64) | collective-permute-done | bytes 540704 | tf_op jit(solution)/shard_map/ppermute | solution.py:418
  55.7 0.7 join0.1
  56.4 4.8 %collective-permute-start.65 = (bf16[528,384]{1,0:T(8,128)(2,1)S(1)}, bf16[528,384]{1,0:T(8,128)(2,1)S(1)}, u32[]{:S(2)}, u32[]{:S(2)}) collective-permute-start(bf16[528,384]{1,0:T(8,128)(2,1)S(1)} %join0.1), channel_id=1, source_target_pairs={{0,4},{1,5},{2,6},{3,7},{4,0},{5,1},{6,2},{7,3},{8,12},{9,13},{10,... | collective-permute-start | bytes 1216520 | tf_op jit(solution)/shard_map/ppermute | solution.py:421
  61.3 3.1 %join1.1 = (bf16[528,384]{1,0:T(8,128)(2,1)S(1)}, bf16[528,384]{1,0:T(8,128)(2,1)S(1)}, bf16[528,384]{1,0:T(8,128)(2,1)S(1)}) custom-call(bf16[528,512]{1,0:T(8,128)(2,1)S(1)} %get-tuple-element.1965.own_ref, bf16[528,512]{1,0:T(8,128)(2,1)S(1)} %collective-permute-done.64.other_ref, bf16[4,512,384]{2,1,0:T(8,128)(2,1)S(1)} %get-tuple-element.1962.refs_0_.refs_1_.refs_2_, ...), custom_call_target="tpu_custom_call" | custom-call | flops 1245708288 | bytes 3440640 | tf_op jit(solution)/shard_map/join1/pallas_call | solution.py:298
  64.4 2.3 %collective-permute-start.66 = (bf16[528,384]{1,0:T(8,128)(2,1)S(1)}, bf16[528,384]{1,0:T(8,128)(2,1)S(1)}, u32[]{:S(2)}, u32[]{:S(2)}) collective-permute-start(bf16[528,384]{1,0:T(8,128)(2,1)S(1)} %get-tuple-element.1967), channel_id=1, source_target_pairs={{0,2},{1,3},{2,4},{3,5},{4,6},{5,7},{6,0},{7,1},{8,10},{9,11},{10,... | collective-permute-start | bytes 1216520 | tf_op jit(solution)/shard_map/ppermute | solution.py:421
  66.7 4.2 %collective-permute-start.67 = (bf16[528,384]{1,0:T(8,128)(2,1)S(1)}, bf16[528,384]{1,0:T(8,128)(2,1)S(1)}, u32[]{:S(2)}, u32[]{:S(2)}) collective-permute-start(bf16[528,384]{1,0:T(8,128)(2,1)S(1)} %get-tuple-element.1968), channel_id=1, source_target_pairs={{0,6},{1,7},{2,0},{3,1},{4,2},{5,3},{6,4},{7,5},{8,14},{9,15},{10,... | collective-permute-start | bytes 1216520 | tf_op jit(solution)/shard_map/ppermute | solution.py:421
  70.9 0.0 collective-permute-done.65.a_ref
  70.9 0.1 add.3.a_ref
  71.0 8.5 %collective-permute-done.66.b_ref = bf16[528,384]{1,0:T(8,128)(2,1)S(1)} collective-permute-done((bf16[528,384]{1,0:T(8,128)(2,1)S(1)}, bf16[528,384]{1,0:T(8,128)(2,1)S(1)}, u32[]{:S(2)}, u32[]{:S(2)}) %collective-permute-start.66) | collective-permute-done | bytes 405536 | tf_op jit(solution)/shard_map/ppermute | solution.py:421
  79.5 0.0 collective-permute-done.67.c_ref
  79.5 0.9 %finish.1 = (bf16[512,384]{1,0:T(8,128)(2,1)}, bf16[2,4,384]{2,1,0:T(4,128)(2,1)}) custom-call(f32[528,384]{1,0:T(8,128)S(1)} %add.3.a_ref, bf16[528,384]{1,0:T(8,128)(2,1)S(1)} %collective-permute-done.66.b_ref, bf16[528,384]{1,0:T(8,128)(2,1)S(1)} %collective-permute-done.67.c_ref), custom_call_target="tpu_custom_call" | custom-call | tf_op jit(solution)/shard_map/finish/pallas_call | solution.py:339
Async XLA Ops:
  0.6 11.8 %copy-start.6 = (s32[64]{0:T(128)S(1)}, s32[64]{0:T(128)}, u32[]{:S(2)}) copy-start(s32[64]{0:T(128)} %partner_ref.1) | copy-start | bytes 772
  0.6 11.8 %copy-start.9 = (f32[4]{0:T(128)S(1)}, f32[4]{0:T(128)}, u32[]{:S(2)}) copy-start(f32[4]{0:T(128)} %slopes_ref.1) | copy-start | bytes 52
  0.7 11.8 %copy-start.3 = (bf16[2,4,512]{2,1,0:T(4,128)(2,1)S(1)}, bf16[2,4,512]{2,1,0:T(4,128)(2,1)}, u32[]{:S(2)}) copy-start(bf16[2,4,512]{2,1,0:T(4,128)(2,1)} %qd_ref.1) | copy-start | bytes 24580
  0.7 11.8 %copy-start = (bf16[512,512]{1,0:T(8,128)(2,1)S(1)}, bf16[512,512]{1,0:T(8,128)(2,1)}, u32[]{:S(2)}) copy-start(bf16[512,512]{1,0:T(8,128)(2,1)} %q_ref.1) | copy-start | bytes 1572868
  0.7 11.8 %copy-start.8 = (s32[1,4]{1,0:T(1,128)S(1)}, s32[1,4]{1,0:T(1,128)}, u32[]{:S(2)}) copy-start(s32[1,4]{1,0:T(1,128)} %decode_ref.1) | copy-start | bytes 52
  0.7 11.8 %copy-start.7 = (s32[64]{0:T(128)S(1)}, s32[64]{0:T(128)}, u32[]{:S(2)}) copy-start(s32[64]{0:T(128)} %count_ref.1) | copy-start | bytes 772
  0.7 11.8 %copy-start.5 = (bf16[2,4,512]{2,1,0:T(4,128)(2,1)S(1)}, bf16[2,4,512]{2,1,0:T(4,128)(2,1)}, u32[]{:S(2)}) copy-start(bf16[2,4,512]{2,1,0:T(4,128)(2,1)} %param.125) | copy-start | bytes 24580
  0.7 11.8 %copy-start.4 = (bf16[2,4,512]{2,1,0:T(4,128)(2,1)S(1)}, bf16[2,4,512]{2,1,0:T(4,128)(2,1)}, u32[]{:S(2)}) copy-start(bf16[2,4,512]{2,1,0:T(4,128)(2,1)} %param.124) | copy-start | bytes 24580
  0.7 11.8 %copy-start.2 = (bf16[512,512]{1,0:T(8,128)(2,1)S(1)}, bf16[512,512]{1,0:T(8,128)(2,1)}, u32[]{:S(2)}) copy-start(bf16[512,512]{1,0:T(8,128)(2,1)} %param.122) | copy-start | bytes 1572868
  0.7 11.8 %copy-start.1 = (bf16[512,512]{1,0:T(8,128)(2,1)S(1)}, bf16[512,512]{1,0:T(8,128)(2,1)}, u32[]{:S(2)}) copy-start(bf16[512,512]{1,0:T(8,128)(2,1)} %param.121) | copy-start | bytes 1572868
  3.4 9.1 %collective-permute-start = (bf16[2,4,128,128]{3,2,1,0:T(8,128)(2,1)S(1)}, bf16[2,4,128,128]{3,2,1,0:T(8,128)(2,1)}, u32[]{:S(2)}, u32[]{:S(2)}) collective-permute-start(bf16[2,4,128,128]{3,2,1,0:T(8,128)(2,1)S(1)} %pack.3), channel_id=1, source_target_pairs={{0,384},{8,392},{16,400},{24,408},{32,416},{40,424},{48,432},{56,4... | collective-permute-start | bytes 786440 | tf_op jit(solution)/shard_map/cond/branch_1_fun/ppermute | solution.py:362
  12.8 36.4 %collective-permute-start.63 = (bf16[2,4,128,128]{3,2,1,0:T(8,128)(2,1)}, bf16[2,4,128,128]{3,2,1,0:T(8,128)(2,1)}, u32[]{:S(2)}, u32[]{:S(2)}) collective-permute-start(bf16[2,4,128,128]{3,2,1,0:T(8,128)(2,1)} %get-tuple-element.1919), channel_id=1, source_target_pairs={{0,248},{8,240},{16,232},{24,224},{32,216},{40,208},{48,200},{56,1... | collective-permute-start | bytes 786440 | tf_op jit(solution)/shard_map/cond/branch_31_fun/ppermute | solution.py:362
  35.7 7.1 %collective-permute-start.62 = (bf16[4,512,384]{2,1,0:T(8,128)(2,1)}, bf16[4,512,384]{2,1,0:T(8,128)(2,1)}, u32[]{:S(2)}, u32[]{:S(2)}) collective-permute-start(bf16[4,512,384]{2,1,0:T(8,128)(2,1)} %param.96), channel_id=1, source_target_pairs={{0,1},{1,0},{2,3},{3,2},{4,5},{5,4},{6,7},{7,6},{8,9},{9,8},{10,11... | collective-permute-start | bytes 4718600 | tf_op jit(solution)/shard_map/cond/branch_31_fun/cond/branch_1_fun/ppermute | solution.py:356
  51.3 4.5 %collective-permute-start.64 = (bf16[528,512]{1,0:T(8,128)(2,1)S(1)}, bf16[528,512]{1,0:T(8,128)(2,1)S(1)}, u32[]{:S(2)}, u32[]{:S(2)}) collective-permute-start(bf16[528,512]{1,0:T(8,128)(2,1)S(1)} %get-tuple-element.1965.own_ref), channel_id=1, source_target_pairs={{0,1},{1,0},{2,3},{3,2},{4,5},{5,4},{6,7},{7,6},{8,9},{9,8},{10,11... | collective-permute-start | bytes 1622024 | tf_op jit(solution)/shard_map/ppermute | solution.py:418
  56.4 14.4 %collective-permute-start.65 = (bf16[528,384]{1,0:T(8,128)(2,1)S(1)}, bf16[528,384]{1,0:T(8,128)(2,1)S(1)}, u32[]{:S(2)}, u32[]{:S(2)}) collective-permute-start(bf16[528,384]{1,0:T(8,128)(2,1)S(1)} %join0.1), channel_id=1, source_target_pairs={{0,4},{1,5},{2,6},{3,7},{4,0},{5,1},{6,2},{7,3},{8,12},{9,13},{10,... | collective-permute-start | bytes 1216520 | tf_op jit(solution)/shard_map/ppermute | solution.py:421
  64.4 15.1 %collective-permute-start.66 = (bf16[528,384]{1,0:T(8,128)(2,1)S(1)}, bf16[528,384]{1,0:T(8,128)(2,1)S(1)}, u32[]{:S(2)}, u32[]{:S(2)}) collective-permute-start(bf16[528,384]{1,0:T(8,128)(2,1)S(1)} %get-tuple-element.1967), channel_id=1, source_target_pairs={{0,2},{1,3},{2,4},{3,5},{4,6},{5,7},{6,0},{7,1},{8,10},{9,11},{10,... | collective-permute-start | bytes 1216520 | tf_op jit(solution)/shard_map/ppermute | solution.py:421
  66.7 12.8 %collective-permute-start.67 = (bf16[528,384]{1,0:T(8,128)(2,1)S(1)}, bf16[528,384]{1,0:T(8,128)(2,1)S(1)}, u32[]{:S(2)}, u32[]{:S(2)}) collective-permute-start(bf16[528,384]{1,0:T(8,128)(2,1)S(1)} %get-tuple-element.1968), channel_id=1, source_target_pairs={{0,6},{1,7},{2,0},{3,1},{4,2},{5,3},{6,4},{7,5},{8,14},{9,15},{10,... | collective-permute-start | bytes 1216520 | tf_op jit(solution)/shard_map/ppermute | solution.py:421
